TPU v7x, 256 devices: a whole 4x4x8 slice. The times are simulated.
256 devices in a mesh: dom: 8 (over z), row: 16 (over y, x), col: 2 (over core).
Axes of the slice: x: 4, y: 4, z: 8, core: 2. Of those that a mesh axis runs over, the one named last changes fastest.
Arguments:
- next_inverse: bfloat16 [8, 4096, 4096], P('dom', 'row', 'col'), may hold values from -6 to 6
- next_arrow: bfloat16 [8, 64, 4096], P('dom', None, 'row'), may hold values from -6 to 6
- factor_win: bfloat16 [8, 4096, 3072], P('dom', 'row', 'col'), may hold values from -0.09375 to 0.09375
- factor_rest: bfloat16 [8, 4096, 1024], P('dom', 'row', 'col'), may hold values from -0.09375 to 0.09375
- arrow_win: bfloat16 [8, 64, 3072], P('dom', None, 'col'), may hold values from -0.75 to 0.75
- arrow_rest: bfloat16 [8, 64, 1024], P('dom', None, 'col'), may hold values from -0.75 to 0.75
- tip_inverse: bfloat16 [64, 64], replicated, may hold values from -6 to 6
- base_win: bfloat16 [8, 3072, 3072], P('dom', 'row', 'col'), may hold values from -6 to 6
- base_rest: bfloat16 [8, 3072, 1024], P('dom', 'row', 'col'), may hold values from -6 to 6
Outputs:
- sub_inverse: bfloat16 [8, 4096, 3072], P('dom', 'row', 'col')
- arrow_inverse: bfloat16 [8, 64, 3072], P('dom', None, 'col')
- diag_win: bfloat16 [8, 3072, 3072], P('dom', 'row', 'col')
- diag_rest: bfloat16 [8, 3072, 1024], P('dom', 'row', 'col')
All inputs are finite; a program needn't handle non-finite values.
Results may differ from a plain program's by a relative error of at most 0.0046.
Values may be sent and summed in bfloat16 or wider, within the bound.
A program may use at most 128 MiB of HBM per device.

v0:
```python
import jax
import jax.numpy as jnp
from jax import lax
from jax.sharding import PartitionSpec as P


def shifted(value, axis, steps):
    count = lax.axis_size(axis)
    leading, last = (max(0, -steps), min(count, count - steps))
    return lax.ppermute(value, axis, [(source, source + steps) for source in range(leading, last)])


def contract_first(left, right):
    return lax.dot_general(
        left, right, (((0,), (0,)), ((), ())), preferred_element_type=jnp.float32
    )


def per_device(
    next_inverse,
    next_arrow,
    factor_win,
    factor_rest,
    arrow_win,
    arrow_rest,
    tip_inverse,
    base_win,
    base_rest,
):
    inverse_tile = next_inverse[0]
    arrow_tile = next_arrow[0]
    factor_tile = factor_win[0]
    factor_other = factor_rest[0]
    ratio_tile = arrow_win[0]
    ratio_other = arrow_rest[0]
    factor_column = lax.all_gather(factor_tile, "row", axis=0, tiled=True)
    inverse_next, arrow_next = shifted((inverse_tile, arrow_tile), "dom", -1)
    start_sum = contract_first(arrow_next, ratio_tile)
    x_total = start_sum + jnp.dot(
        lax.all_gather(inverse_next, "col", axis=1, tiled=True),
        factor_column,
        preferred_element_type=jnp.float32,
    )
    x_bf = x_total.astype(jnp.bfloat16)
    y_part = jnp.dot(arrow_next, factor_tile, preferred_element_type=jnp.float32)
    y_total = lax.psum(y_part, "row") + jnp.dot(
        tip_inverse, ratio_tile, preferred_element_type=jnp.float32
    )
    y_bf = y_total.astype(jnp.bfloat16)
    x_panel, y_panel = (
        lax.all_gather(x_bf, "col", axis=1, tiled=True),
        lax.all_gather(y_bf, "col", axis=1, tiled=True),
    )
    ratio_both = jnp.concatenate([ratio_tile, ratio_other], axis=1)
    rows_here = y_panel.shape[1] // lax.axis_size("row")
    y_rows = lax.dynamic_slice_in_dim(y_panel, lax.axis_index("row") * rows_here, rows_here, 1)
    x_columns = lax.all_to_all(x_panel, "row", split_axis=1, concat_axis=0, tiled=True)
    rest_column = lax.all_gather(factor_other, "row", axis=0, tiled=True)
    factor_full = jnp.concatenate([factor_column, rest_column], axis=1)
    diag_part = contract_first(x_columns, factor_full)
    base_both = jnp.concatenate([base_win[0], base_rest[0]], axis=1).astype(jnp.float32)
    diag_total = base_both + diag_part + contract_first(y_rows, ratio_both)
    split = factor_tile.shape[1]
    diag_left = diag_total[:, :split].astype(jnp.bfloat16)
    diag_right = diag_total[:, split:].astype(jnp.bfloat16)
    return ((-x_bf)[None], (-y_bf)[None], diag_left[None], diag_right[None])


def solution(mesh):
    in_specs = (
        P("dom", "row", "col"),
        P("dom", None, "row"),
        P("dom", "row", "col"),
        P("dom", "row", "col"),
        P("dom", None, "col"),
        P("dom", None, "col"),
        P(),
        P("dom", "row", "col"),
        P("dom", "row", "col"),
    )
    out_specs = (
        P("dom", "row", "col"),
        P("dom", None, "col"),
        P("dom", "row", "col"),
        P("dom", "row", "col"),
    )
    return jax.shard_map(
        per_device, mesh=mesh, in_specs=in_specs, out_specs=out_specs, check_vma=False
    )
```

profile of v0, /device:TPU:1, one launch (start us, length us, event | category | flops | bytes accessed | tf_op | source)
XLA Modules:
  0.0 360.3 jit_solution(10407591954021950761)
XLA Ops:
  7.2 0.0 all-gather.7.cloned.1.call-start
  7.2 1.3 collective-permute-start.1
  8.5 24.2 %collective-permute-done.1 = bf16[256,2048]{1,0:T(8,128)(2,1)S(1)} collective-permute-done((bf16[256,2048]{1,0:T(8,128)(2,1)}, bf16[256,2048]{1,0:T(8,128)(2,1)S(1)}, u32[]{:S(2)}, u32[]{:S(2)}) %collective-permute-start.1) | collective-permute-done | bytes 1048608 | tf_op jit(solution)/shard_map/ppermute | solution.py:10
  32.8 1.0 copy-done.4
  33.8 0.0 all-gather.7.cloned.1.call-update
  33.8 0.0 all-gather.11.cloned.1.call-start
  33.9 0.7 all-gather.11.cloned.1.call-update
  34.6 0.0 all-gather.9.cloned.1.call-start
  34.6 1.4 collective-permute-start
  36.1 19.8 %all-gather.7.cloned.1.call-done = bf16[256,4096]{1,0:T(8,128)(2,1)} async-done(((bf16[256,2048]{1,0:T(8,128)(2,1)}), bf16[256,4096]{1,0:T(8,128)(2,1)}) %all-gather.7.cloned.1.call-update) | async-done | bytes 2097168 | tf_op jit(solution)/shard_map/all_gather | solution.py:40
  55.9 98.0 %all-gather.11.cloned.1.call-done = bf16[1,4096,1536]{2,1,0:T(8,128)(2,1)} async-done(((bf16[1,256,1536]{2,1,0:T(8,128)(2,1)}), bf16[1,4096,1536]{2,1,0:T(8,128)(2,1)}) %all-gather.11.cloned.1.call-update) | async-done | bytes 12582928 | tf_op jit(solution)/shard_map/all_gather | solution.py:36
  153.9 7.0 %fusion.18 = f32[256,1536]{1,0:T(8,128)S(1)} fusion(bf16[256,4096]{1,0:T(8,128)(2,1)} %all-gather.7.cloned.1.call-done, bf16[1,4096,1536]{2,1,0:T(8,128)(2,1)} %all-gather.11.cloned.1.call-done), kind=kOutput, calls=%fused_computation.23 | convolution fusion | flops 3221225472 | bytes 16252928 | tf_op jit(solution)/shard_map/dot_general | solution.py:39
  161.0 1.3 fusion.4
  162.3 0.0 all-reduce.2.cloned.1.call-start
  162.3 1.0 fusion.9
  163.3 0.0 all-reduce.2.cloned.1.call-update
  163.3 0.0 all-gather.13.cloned.1.call-start
  163.4 0.5 all-gather.13.cloned.1.call-update
  163.9 14.1 %all-gather.9.cloned.1.call-done = bf16[256,3072]{1,0:T(8,128)(2,1)} async-done(((bf16[256,1536]{1,0:T(8,128)(2,1)}), bf16[256,3072]{1,0:T(8,128)(2,1)}) %all-gather.9.cloned.1.call-update) | async-done | bytes 1572880 | tf_op jit(solution)/shard_map/all_gather | solution.py:51
  178.0 2.6 copy.13
  180.6 6.3 %all-to-all-start = ((bf16[256,16,192]{0,2,1:T(8,128)(2,1)}), bf16[256,16,192]{0,2,1:T(8,128)(2,1)S(1)}, u32[]{:S(2)}, u32[]{:S(2)}) async-start(bf16[256,16,192]{0,2,1:T(8,128)(2,1)} %bitcast.9), calls=%async_computation | async-start | bytes 3145728 | tf_op jit(solution)/shard_map/all_to_all | solution.py:57
  186.9 0.2 fusion.20
  187.1 95.9 %all-reduce.2.cloned.1.call-done = f32[64,1536]{1,0:T(8,128)} async-done(((f32[64,1536]{1,0:T(8,128)}), f32[64,1536]{1,0:T(8,128)}) %all-reduce.2.cloned.1.call-update) | async-done | bytes 393232 | tf_op jit(solution)/shard_map/psum | solution.py:46
  283.0 1.7 negate_bitcast_fusion.1
  284.7 3.8 %all_gather.19 = bf16[64,3072]{1,0:T(8,128)(2,1)} all-gather(bf16[64,1536]{1,0:T(8,128)(2,1)S(1)} %get-tuple-element.5), channel_id=1, replica_groups=mesh['dom'=8,'row'=16,'col'=2] {'col'}, dimensions={1}, use_global_device_ids=true | all-gather | bytes 589824 | tf_op jit(solution)/shard_map/all_gather | solution.py:52
  288.5 0.9 negate_bitcast_fusion
  289.4 0.2 copy.15
  289.6 53.0 %all-gather.13.cloned.1.call-done = bf16[1,4096,512]{2,1,0:T(8,128)(2,1)} async-done(((bf16[1,256,512]{2,1,0:T(8,128)(2,1)}), bf16[1,4096,512]{2,1,0:T(8,128)(2,1)}) %all-gather.13.cloned.1.call-update) | async-done | bytes 4194320 | tf_op jit(solution)/shard_map/all_gather | solution.py:58
  342.6 8.4 %fusion.5 = f32[192,2048]{1,0:T(8,128)S(1)} fusion(bf16[4096,192]{0,1:T(8,128)(2,1)S(1)} %bitcast.36, bf16[4096,512]{1,0:T(8,128)(2,1)} %bitcast.39, bf16[4096,1536]{1,0:T(8,128)(2,1)} %bitcast.38, bf16[192,512]{1,0:T(8,128)(2,1)S(1)} %bitcast.42, bf16[192,1536]{1,0:T(8,128)(2,1)} %bitcast.41), kind=kOutput, calls=%fused_computation.7 | convolution fusion | flops 3256745984 | bytes 20709376 | tf_op jit(solution)/shard_map/dot_general | solution.py:14
  351.0 1.3 fusion.8
  352.2 0.9 slice_bitcast_fusion
  353.1 0.7 slice_bitcast_fusion.1
  (18 shorter events, 0.1 us)
Async XLA Ops:
  7.2 179.7 %copy-start = (bf16[64,64]{1,0:T(8,128)(2,1)S(1)}, bf16[64,64]{1,0:T(8,128)(2,1)}, u32[]{:S(2)}) copy-start(bf16[64,64]{1,0:T(8,128)(2,1)} %param.15) | copy-start | bytes 24580
  7.2 27.4 %copy-start.7 = (bf16[1,64,256]{2,1,0:T(8,128)(2,1)S(1)}, bf16[1,64,256]{2,1,0:T(8,128)(2,1)}, u32[]{:S(2)}) copy-start(bf16[1,64,256]{2,1,0:T(8,128)(2,1)} %param.10) | copy-start | bytes 98308
  7.2 48.7 %all-gather.7.cloned.1.call-start = ((), (), s32[]{:S(2)}) async-start(), calls=%async_computation.1 | async-start | bytes 3145728 | tf_op jit(solution)/shard_map/all_gather | solution.py:40
  7.2 25.5 %collective-permute-start.1 = (bf16[256,2048]{1,0:T(8,128)(2,1)}, bf16[256,2048]{1,0:T(8,128)(2,1)S(1)}, u32[]{:S(2)}, u32[]{:S(2)}) collective-permute-start(bf16[256,2048]{1,0:T(8,128)(2,1)} %bitcast.40), channel_id=1, source_target_pairs={{32,0},{64,32},{96,64},{128,96},{160,128},{192,160},{224,192},{33,... | collective-permute-start | bytes 3145736 | tf_op jit(solution)/shard_map/ppermute | solution.py:10
  32.8 1.0 copy-start.4
  33.8 120.1 %all-gather.11.cloned.1.call-start = ((), (), s32[]{:S(2)}) async-start(), calls=%async_computation.4 | async-start | bytes 13369344 | tf_op jit(solution)/shard_map/all_gather | solution.py:36
  34.6 143.5 %all-gather.9.cloned.1.call-start = ((), (), s32[]{:S(2)}) async-start(), calls=%async_computation.3 | async-start | bytes 2359296 | tf_op jit(solution)/shard_map/all_gather | solution.py:51
  34.6 126.3 %copy-start.3 = (bf16[1,64,1536]{2,1,0:T(8,128)(2,1)S(1)}, bf16[1,64,1536]{2,1,0:T(8,128)(2,1)}, u32[]{:S(2)}) copy-start(bf16[1,64,1536]{2,1,0:T(8,128)(2,1)} %param.13) | copy-start | bytes 589828
  34.6 126.3 %collective-permute-start = (bf16[64,256]{1,0:T(8,128)(2,1)S(1)}, bf16[64,256]{1,0:T(8,128)(2,1)S(1)}, u32[]{:S(2)}, u32[]{:S(2)}) collective-permute-start(bf16[64,256]{1,0:T(8,128)(2,1)S(1)} %bitcast.43), channel_id=1, source_target_pairs={{32,0},{64,32},{96,64},{128,96},{160,128},{192,160},{224,192},{33,... | collective-permute-start | bytes 98312 | tf_op jit(solution)/shard_map/ppermute | solution.py:10
  160.9 1.4 copy-start.2
  162.3 120.7 %all-reduce.2.cloned.1.call-start = ((), (), s32[]{:S(2)}) async-start(), calls=%async_computation.2 | async-start | bytes 786432 | tf_op jit(solution)/shard_map/psum | solution.py:46
  163.3 179.2 %all-gather.13.cloned.1.call-start = ((), (), s32[]{:S(2)}) async-start(), calls=%async_computation.5 | async-start | bytes 4456448 | tf_op jit(solution)/shard_map/all_gather | solution.py:58
  180.6 108.8 %all-to-all-start = ((bf16[256,16,192]{0,2,1:T(8,128)(2,1)}), bf16[256,16,192]{0,2,1:T(8,128)(2,1)S(1)}, u32[]{:S(2)}, u32[]{:S(2)}) async-start(bf16[256,16,192]{0,2,1:T(8,128)(2,1)} %bitcast.9), calls=%async_computation | async-start | bytes 3145728 | tf_op jit(solution)/shard_map/all_to_all | solution.py:57
  186.9 101.6 %copy-start.1 = (bf16[256,1536]{1,0:T(8,128)(2,1)S(1)}, bf16[256,1536]{1,0:T(8,128)(2,1)}, u32[]{:S(2)}) copy-start(bf16[256,1536]{1,0:T(8,128)(2,1)} %fusion.4) | copy-start | bytes 2359300
  289.4 53.1 %copy-start.6 = (bf16[1,192,512]{2,1,0:T(8,128)(2,1)S(1)}, bf16[1,192,512]{2,1,0:T(8,128)(2,1)}, u32[]{:S(2)}) copy-start(bf16[1,192,512]{2,1,0:T(8,128)(2,1)} %param.17) | copy-start | bytes 589828
  342.6 8.4 %copy-start.5 = (bf16[1,64,512]{2,1,0:T(8,128)(2,1)S(1)}, bf16[1,64,512]{2,1,0:T(8,128)(2,1)}, u32[]{:S(2)}) copy-start(bf16[1,64,512]{2,1,0:T(8,128)(2,1)} %param.14) | copy-start | bytes 196612
Sparse Core Ops, SparseCore 0:
  33.9 21.8 all-gather.6
  58.3 95.5 all-gather.10
  162.4 15.6 all-gather.8
  181.7 101.2 all-reduce.1
  285.3 57.2 all-gather.12
where the time goes:
time: 361 us; the launch traced here: 360 us
  waiting for transfers between devices  306 us (85%)
  matrix products  19.1 us (5%)
  between operations  13.9 us (4%)
  starting transfers between devices  9.18 us (3%)
  local copies, waits for them, and re-layouts  5.35 us (1%)
  blocking collectives  3.8 us (1%)
    all_gather x1, waiting for transfers between devices, per_device(): factor_column = lax.all_gather(factor_tile, 'row', axis=0, tiled=True)  98 us
    psum x1, waiting for transfers between devices, per_device(): lax.psum(y_part, 'row')  95.9 us
    all_gather x1, waiting for transfers between devices, per_device(): rest_column = lax.all_gather(factor_other, 'row', axis=0, tiled=True)  53 us
    ppermute x2, waiting for transfers between devices, shifted(): lax.ppermute(value, axis, [(source, source + steps) for source in range(l...  24.2 us
    all_gather x1, waiting for transfers between devices, per_device(): lax.all_gather(inverse_next, 'col', axis=1, tiled=True)  19.8 us
    all_gather x1, waiting for transfers between devices, per_device(): lax.all_gather(x_bf, 'col', axis=1, tiled=True)  14.1 us
    dot_general x3, matrix products, contract_first(): lax.dot_general(left, right, (((0,), (0,)), ((), ())), preferred_element_...  10.9 us
  transfers between devices with their start and end apart: 8, of which 6 were waited for; matrix products, arithmetic and copies ran while one was open for 4% of the time, Pallas kernels for 0%

commit v1 on v0

--- a/solution.py
+++ b/solution.py
@@ -2,6 +2,11 @@
 import jax.numpy as jnp
 from jax import lax
 from jax.sharding import PartitionSpec as P
+
+
+def summed_here(array, axis):
+    pieces = lax.all_gather(array, axis)
+    return jnp.sum(pieces, axis=0)
 
 
 def shifted(value, axis, steps):
@@ -43,7 +48,7 @@
     )
     x_bf = x_total.astype(jnp.bfloat16)
     y_part = jnp.dot(arrow_next, factor_tile, preferred_element_type=jnp.float32)
-    y_total = lax.psum(y_part, "row") + jnp.dot(
+    y_total = summed_here(y_part, "row") + jnp.dot(
         tip_inverse, ratio_tile, preferred_element_type=jnp.float32
     )
     y_bf = y_total.astype(jnp.bfloat16)

time: 361 us -> 334 us (0.925)
  waiting for transfers between devices: 306 us -> 278 us
    psum x1 -> x0, waiting for transfers between devices: 95.9 us -> none  [per_device(): lax.psum(y_part, 'row')]
    all_gather x0 -> x1, waiting for transfers between devices: none -> 70.2 us  [summed_here(): pieces = lax.all_gather(array, axis)]
  transfers between devices with their start and end apart: 8 -> 8, of which waited for: 6 -> 6; matrix products, arithmetic and copies ran while one was open for 4% -> 5% of each run, Pallas kernels for 0% -> 0%
where the time goes in v1:
time: 334 us
  waiting for transfers between devices  278 us (83%)
  matrix products  19.1 us (6%)
  between operations  13.9 us (4%)
  starting transfers between devices  9.18 us (3%)
  local copies, waits for them, and re-layouts  5.39 us (2%)
  other arithmetic  4.83 us (1%)
    all_gather x1, waiting for transfers between devices, per_device(): factor_column = lax.all_gather(factor_tile, 'row', axis=0, tiled=True)  98 us
    all_gather x1, waiting for transfers between devices, summed_here(): pieces = lax.all_gather(array, axis)  70.2 us
    all_gather x1, waiting for transfers between devices, per_device(): rest_column = lax.all_gather(factor_other, 'row', axis=0, tiled=True)  50.7 us
    ppermute x2, waiting for transfers between devices, shifted(): lax.ppermute(value, axis, [(source, source + steps) for source in range(l...  24.2 us
    all_gather x1, waiting for transfers between devices, per_device(): lax.all_gather(inverse_next, 'col', axis=1, tiled=True)  19.8 us
    all_gather x1, waiting for transfers between devices, per_device(): lax.all_gather(x_bf, 'col', axis=1, tiled=True)  14.1 us
    dot_general x3, matrix products, contract_first(): lax.dot_general(left, right, (((0,), (0,)), ((), ())), preferred_element_...  10.9 us
    dot_general x1, matrix products, per_device(): jnp.dot(lax.all_gather(inverse_next, 'col', axis=1, tiled=True), factor_c...  7.04 us
  transfers between devices with their start and end apart: 8, of which 6 were waited for; matrix products, arithmetic and copies ran while one was open for 5% of the time, Pallas kernels for 0%

profile of v1, /device:TPU:1, one launch (start us, length us, event | category | flops | bytes accessed | tf_op | source)
XLA Modules:
  0.0 333.5 jit_solution(8709053575254865340)
XLA Ops:
  7.2 0.0 all-gather.9.cloned.1.call-start
  7.2 1.3 collective-permute-start.1
  8.5 24.2 %collective-permute-done.1 = bf16[256,2048]{1,0:T(8,128)(2,1)S(1)} collective-permute-done((bf16[256,2048]{1,0:T(8,128)(2,1)}, bf16[256,2048]{1,0:T(8,128)(2,1)S(1)}, u32[]{:S(2)}, u32[]{:S(2)}) %collective-permute-start.1) | collective-permute-done | bytes 1048608 | tf_op jit(solution)/shard_map/ppermute | solution.py:15
  32.8 1.0 copy-done.4
  33.8 0.0 all-gather.9.cloned.1.call-update
  33.8 0.0 all-gather.13.cloned.1.call-start
  33.8 0.7 all-gather.13.cloned.1.call-update
  34.5 0.0 all-gather.11.cloned.1.call-start
  34.6 1.4 collective-permute-start
  36.0 19.8 %all-gather.9.cloned.1.call-done = bf16[256,4096]{1,0:T(8,128)(2,1)} async-done(((bf16[256,2048]{1,0:T(8,128)(2,1)}), bf16[256,4096]{1,0:T(8,128)(2,1)}) %all-gather.9.cloned.1.call-update) | async-done | bytes 2097168 | tf_op jit(solution)/shard_map/all_gather | solution.py:45
  55.9 98.0 %all-gather.13.cloned.1.call-done = bf16[1,4096,1536]{2,1,0:T(8,128)(2,1)} async-done(((bf16[1,256,1536]{2,1,0:T(8,128)(2,1)}), bf16[1,4096,1536]{2,1,0:T(8,128)(2,1)}) %all-gather.13.cloned.1.call-update) | async-done | bytes 12582928 | tf_op jit(solution)/shard_map/all_gather | solution.py:41
  153.9 7.0 %fusion.19 = f32[256,1536]{1,0:T(8,128)S(1)} fusion(bf16[256,4096]{1,0:T(8,128)(2,1)} %all-gather.9.cloned.1.call-done, bf16[1,4096,1536]{2,1,0:T(8,128)(2,1)} %all-gather.13.cloned.1.call-done), kind=kOutput, calls=%fused_computation.24 | convolution fusion | flops 3221225472 | bytes 16252928 | tf_op jit(solution)/shard_map/dot_general | solution.py:44
  161.0 1.3 fusion.4
  162.3 0.0 all-gather.15.cloned.1.call-start
  162.3 1.0 fusion.10
  163.4 0.0 all-gather.17.cloned.1.call-start
  163.4 0.5 all-gather.17.cloned.1.call-update
  163.9 14.1 %all-gather.11.cloned.1.call-done = bf16[256,3072]{1,0:T(8,128)(2,1)} async-done(((bf16[256,1536]{1,0:T(8,128)(2,1)}), bf16[256,3072]{1,0:T(8,128)(2,1)}) %all-gather.11.cloned.1.call-update) | async-done | bytes 1572880 | tf_op jit(solution)/shard_map/all_gather | solution.py:56
  178.0 2.6 copy.13
  180.7 6.3 %all-to-all-start = ((bf16[256,16,192]{0,2,1:T(8,128)(2,1)}), bf16[256,16,192]{0,2,1:T(8,128)(2,1)S(1)}, u32[]{:S(2)}, u32[]{:S(2)}) async-start(bf16[256,16,192]{0,2,1:T(8,128)(2,1)} %bitcast.10), calls=%async_computation | async-start | bytes 3145728 | tf_op jit(solution)/shard_map/all_to_all | solution.py:62
  186.9 70.2 %all-gather.15.cloned.1.call-done = f32[1024,1536]{1,0:T(8,128)} async-done(((f32[64,1536]{1,0:T(8,128)}), f32[1024,1536]{1,0:T(8,128)}) %all-gather.15.cloned.1.call-update) | async-done | bytes 6291472 | tf_op jit(solution)/shard_map/all_gather | solution.py:8
  257.2 3.2 reduce_sum.9
  260.4 0.2 fusion.9
  260.6 2.7 all_gather.27
  263.2 0.7 negate_bitcast_fusion.1
  263.9 0.9 negate_bitcast_fusion
  264.9 0.2 copy.15
  265.0 50.7 %all-gather.17.cloned.1.call-done = bf16[1,4096,512]{2,1,0:T(8,128)(2,1)} async-done(((bf16[1,256,512]{2,1,0:T(8,128)(2,1)}), bf16[1,4096,512]{2,1,0:T(8,128)(2,1)}) %all-gather.17.cloned.1.call-update) | async-done | bytes 4194320 | tf_op jit(solution)/shard_map/all_gather | solution.py:63
  315.8 8.4 %fusion.5 = f32[192,2048]{1,0:T(8,128)S(1)} fusion(bf16[4096,192]{0,1:T(8,128)(2,1)S(1)} %bitcast.38, bf16[4096,512]{1,0:T(8,128)(2,1)} %bitcast.41, bf16[4096,1536]{1,0:T(8,128)(2,1)} %bitcast.40, bf16[192,512]{1,0:T(8,128)(2,1)S(1)} %bitcast.44, bf16[192,1536]{1,0:T(8,128)(2,1)} %bitcast.43), kind=kOutput, calls=%fused_computation.7 | convolution fusion | flops 3256745984 | bytes 20709376 | tf_op jit(solution)/shard_map/dot_general | solution.py:19
  324.1 1.3 fusion.8
  325.4 0.9 slice_bitcast_fusion
  326.3 0.7 slice_bitcast_fusion.1
  (19 shorter events, 0.1 us)
Async XLA Ops:
  7.2 253.2 %copy-start = (bf16[64,64]{1,0:T(8,128)(2,1)S(1)}, bf16[64,64]{1,0:T(8,128)(2,1)}, u32[]{:S(2)}) copy-start(bf16[64,64]{1,0:T(8,128)(2,1)} %param.15) | copy-start | bytes 24580
  7.2 27.4 %copy-start.7 = (bf16[1,64,256]{2,1,0:T(8,128)(2,1)S(1)}, bf16[1,64,256]{2,1,0:T(8,128)(2,1)}, u32[]{:S(2)}) copy-start(bf16[1,64,256]{2,1,0:T(8,128)(2,1)} %param.10) | copy-start | bytes 98308
  7.2 48.7 %all-gather.9.cloned.1.call-start = ((), (), s32[]{:S(2)}) async-start(), calls=%async_computation.1 | async-start | bytes 3145728 | tf_op jit(solution)/shard_map/all_gather | solution.py:45
  7.2 25.5 %collective-permute-start.1 = (bf16[256,2048]{1,0:T(8,128)(2,1)}, bf16[256,2048]{1,0:T(8,128)(2,1)S(1)}, u32[]{:S(2)}, u32[]{:S(2)}) collective-permute-start(bf16[256,2048]{1,0:T(8,128)(2,1)} %bitcast.42), channel_id=1, source_target_pairs={{32,0},{64,32},{96,64},{128,96},{160,128},{192,160},{224,192},{33,... | collective-permute-start | bytes 3145736 | tf_op jit(solution)/shard_map/ppermute | solution.py:15
  32.8 1.0 copy-start.4
  33.8 120.1 %all-gather.13.cloned.1.call-start = ((), (), s32[]{:S(2)}) async-start(), calls=%async_computation.3 | async-start | bytes 13369344 | tf_op jit(solution)/shard_map/all_gather | solution.py:41
  34.5 143.5 %all-gather.11.cloned.1.call-start = ((), (), s32[]{:S(2)}) async-start(), calls=%async_computation.2 | async-start | bytes 2359296 | tf_op jit(solution)/shard_map/all_gather | solution.py:56
  34.6 126.4 %copy-start.3 = (bf16[1,64,1536]{2,1,0:T(8,128)(2,1)S(1)}, bf16[1,64,1536]{2,1,0:T(8,128)(2,1)}, u32[]{:S(2)}) copy-start(bf16[1,64,1536]{2,1,0:T(8,128)(2,1)} %param.13) | copy-start | bytes 589828
  34.6 126.3 %collective-permute-start = (bf16[64,256]{1,0:T(8,128)(2,1)S(1)}, bf16[64,256]{1,0:T(8,128)(2,1)S(1)}, u32[]{:S(2)}, u32[]{:S(2)}) collective-permute-start(bf16[64,256]{1,0:T(8,128)(2,1)S(1)} %bitcast.45), channel_id=1, source_target_pairs={{32,0},{64,32},{96,64},{128,96},{160,128},{192,160},{224,192},{33,... | collective-permute-start | bytes 98312 | tf_op jit(solution)/shard_map/ppermute | solution.py:15
  160.9 1.4 copy-start.2
  162.3 94.9 %all-gather.15.cloned.1.call-start = ((), (), s32[]{:S(2)}) async-start(), calls=%async_computation.4 | async-start | bytes 6684672 | tf_op jit(solution)/shard_map/all_gather | solution.py:8
  163.4 152.4 %all-gather.17.cloned.1.call-start = ((), (), s32[]{:S(2)}) async-start(), calls=%async_computation.5 | async-start | bytes 4456448 | tf_op jit(solution)/shard_map/all_gather | solution.py:63
  180.7 84.2 %all-to-all-start = ((bf16[256,16,192]{0,2,1:T(8,128)(2,1)}), bf16[256,16,192]{0,2,1:T(8,128)(2,1)S(1)}, u32[]{:S(2)}, u32[]{:S(2)}) async-start(bf16[256,16,192]{0,2,1:T(8,128)(2,1)} %bitcast.10), calls=%async_computation | async-start | bytes 3145728 | tf_op jit(solution)/shard_map/all_to_all | solution.py:62
  260.4 3.5 %copy-start.1 = (bf16[256,1536]{1,0:T(8,128)(2,1)S(1)}, bf16[256,1536]{1,0:T(8,128)(2,1)}, u32[]{:S(2)}) copy-start(bf16[256,1536]{1,0:T(8,128)(2,1)} %fusion.4) | copy-start | bytes 2359300
  264.9 50.9 %copy-start.6 = (bf16[1,192,512]{2,1,0:T(8,128)(2,1)S(1)}, bf16[1,192,512]{2,1,0:T(8,128)(2,1)}, u32[]{:S(2)}) copy-start(bf16[1,192,512]{2,1,0:T(8,128)(2,1)} %param.17) | copy-start | bytes 589828
  315.8 8.4 %copy-start.5 = (bf16[1,64,512]{2,1,0:T(8,128)(2,1)S(1)}, bf16[1,64,512]{2,1,0:T(8,128)(2,1)}, u32[]{:S(2)}) copy-start(bf16[1,64,512]{2,1,0:T(8,128)(2,1)} %param.14) | copy-start | bytes 196612
Sparse Core Ops, SparseCore 0:
  33.9 21.8 all-gather.8
  58.3 95.5 all-gather.12
  162.4 15.5 all-gather.10
  180.9 76.2 all-gather.14
  259.4 56.2 all-gather.16
